TPU v7x, 32 devices: a whole 2x2x4 slice. The times are simulated.
32 devices in a mesh: ctx: 16 (over z, y, core), head: 2 (over x).
Axes of the slice: x: 2, y: 2, z: 4, core: 2. Of those that a mesh axis runs over, the one named last changes fastest.
Arguments:
- queries: bfloat16 [2048, 2048], P('ctx', 'head'), may hold values from -6 to 6
- key_states: bfloat16 [2048, 512], P(('ctx', 'head')), may hold values from -6 to 6
- value_states: bfloat16 [2048, 512], P(('ctx', 'head')), may hold values from -6 to 6
- attn_out: bfloat16 [2048, 2048], P('ctx', 'head'), may hold values from -1.5 to 1.5
- grad_out: bfloat16 [2048, 2048], P('ctx', 'head'), may hold values from -24 to 24
- log_sum_exp: float32 [16, 2048], P('head', 'ctx')
- token_order: int32 [2048], P('ctx'), may hold values from 0 to 2047, as said below
- position: int32 [2048], P('ctx'), may hold values from 0 to 511, as said below
Outputs:
- grad_queries: bfloat16 [2048, 2048], P('ctx', 'head')
- grad_keys: bfloat16 [2048, 512], P(('ctx', 'head'))
- grad_values: bfloat16 [2048, 512], P(('ctx', 'head'))
Inputs may be any that keep to these rules, and one draw needn't show every extreme that they name: `token_order`: a permutation of the sequence positions; the 128 rows of ctx index d hold consecutive positions in increasing order, all within quarter d mod 4 of the sequence (quarter k holds positions k * 512 to (k + 1) * 512 - 1). Documents are runs of consecutive sequence positions that never cross a multiple of 512; token_order[r] - position[r] is the sequence position where row r's document starts; some document fills a whole quarter.
All inputs are finite; a program needn't handle non-finite values.
Results may differ from a plain program's by a relative error of at most 0.0055.
Values may be sent and summed in bfloat16 or wider, within the bound.
A program may use at most 64 MiB of HBM per device.

v0:
```python
import jax
import jax.numpy as jnp
from jax import lax
from jax.sharding import PartitionSpec as P

HEAD_DIM = 128


def from_behind(value, axis, steps):
    count = lax.axis_size(axis)
    pairs = [(source, (source + steps) % count) for source in range(count)]
    return lax.ppermute(value, axis, pairs)


def block_grads(query_side, keys, values, key_order):
    queries, grads, lse_rows, dot_rows, query_first, query_last = query_side
    row_count = queries.shape[0]
    span = keys.shape[0]
    kv_local = keys.shape[1] // HEAD_DIM
    group_size = queries.shape[1] // HEAD_DIM // kv_local
    score_scale = HEAD_DIM ** (-0.5)
    query_four = queries.reshape(row_count, kv_local, group_size, HEAD_DIM)
    grad_four = grads.reshape(row_count, kv_local, group_size, HEAD_DIM)
    keys_three = keys.reshape(span, kv_local, HEAD_DIM)
    values_three = values.reshape(span, kv_local, HEAD_DIM)
    visible = (key_order[None, :] <= query_last[:, None]) & (
        key_order[None, :] >= query_first[:, None]
    )
    scores = (
        jnp.einsum("tkgd,nkd->kgtn", query_four, keys_three, preferred_element_type=jnp.float32)
        * score_scale
    )
    lse_three = lse_rows.reshape(kv_local, group_size, row_count)
    weights = jnp.where(visible[None, None], jnp.exp(scores - lse_three[..., None]), 0.0)
    prob_grad = jnp.einsum(
        "tkgd,nkd->kgtn", grad_four, values_three, preferred_element_type=jnp.float32
    )
    dot_three = dot_rows.reshape(kv_local, group_size, row_count)
    score_grad = (weights * (prob_grad - dot_three[..., None]) * score_scale).astype(jnp.bfloat16)
    weights_round = weights.astype(jnp.bfloat16)
    query_update = jnp.einsum(
        "kgtn,nkd->tkgd", score_grad, keys_three, preferred_element_type=jnp.float32
    )
    key_update = jnp.einsum(
        "kgtn,tkgd->nkd", score_grad, query_four, preferred_element_type=jnp.float32
    )
    value_update = jnp.einsum(
        "kgtn,tkgd->nkd", weights_round, grad_four, preferred_element_type=jnp.float32
    )
    return (
        query_update.reshape(row_count, -1),
        key_update.reshape(span, -1),
        value_update.reshape(span, -1),
    )


def visit(query_side, state, keys, values, key_order):
    query_update, key_update, value_update = block_grads(query_side, keys, values, key_order)
    return (state[0] + query_update, state[1] + key_update, state[2] + value_update)


def shards(
    queries, key_states, value_states, attn_out, grad_out, log_sum_exp, token_order, position
):
    row_count = queries.shape[0]
    head_columns = queries.shape[1]
    local_heads = log_sum_exp.shape[0]
    product = grad_out.astype(jnp.float32) * attn_out.astype(jnp.float32)
    out_dot = jnp.sum(product.reshape(row_count, local_heads, HEAD_DIM), axis=2)
    query_side = (
        queries,
        grad_out,
        log_sum_exp,
        jnp.transpose(out_dot),
        token_order - position,
        token_order,
    )
    all_starts = lax.all_gather(token_order[:1], "ctx", axis=0, tiled=True)
    key_mine, value_mine = (
        lax.all_to_all(key_states, "head", split_axis=1, concat_axis=0, tiled=True),
        lax.all_to_all(value_states, "head", split_axis=1, concat_axis=0, tiled=True),
    )
    kv_columns = key_mine.shape[1]
    ctx_count = lax.axis_size("ctx")
    here = lax.axis_index("ctx")
    hops = ctx_count // 4
    query_zero = jnp.zeros((row_count, head_columns), jnp.float32)

    def order_rows(source, first, count):
        start_value = lax.dynamic_index_in_dim(all_starts, source, 0, keepdims=False)
        return start_value + first + jnp.arange(count, dtype=jnp.int32)

    grad_zero = jnp.zeros((row_count, kv_columns), jnp.float32)
    query_sum, key_grad, value_grad = visit(
        query_side, (query_zero, grad_zero, grad_zero), key_mine, value_mine, token_order
    )

    def hop_one(step, state):
        query_sum, keys, values, key_grad, value_grad = state
        keys, values = from_behind((keys, values), "ctx", 4)
        key_grad, value_grad = from_behind((key_grad, value_grad), "ctx", 4)
        source = (here - 4 * step) % ctx_count
        query_sum, key_grad, value_grad = visit(
            query_side,
            (query_sum, key_grad, value_grad),
            keys,
            values,
            order_rows(source, 0, row_count),
        )
        return (query_sum, keys, values, key_grad, value_grad)

    state = lax.fori_loop(1, hops, hop_one, (query_sum, key_mine, value_mine, key_grad, value_grad))
    query_sum = state[0]
    key_grad, value_grad = (
        from_behind(state[3].astype(jnp.bfloat16), "ctx", 4).astype(jnp.float32),
        from_behind(state[4].astype(jnp.bfloat16), "ctx", 4).astype(jnp.float32),
    )
    grad_queries = query_sum.astype(jnp.bfloat16)
    grad_keys, grad_values = (
        lax.all_to_all(
            key_grad.astype(jnp.bfloat16), "head", split_axis=0, concat_axis=1, tiled=True
        ),
        lax.all_to_all(
            value_grad.astype(jnp.bfloat16), "head", split_axis=0, concat_axis=1, tiled=True
        ),
    )
    return (grad_queries, grad_keys, grad_values)


def solution(mesh):
    in_specs = (
        P("ctx", "head"),
        P(("ctx", "head"), None),
        P(("ctx", "head"), None),
        P("ctx", "head"),
        P("ctx", "head"),
        P("head", "ctx"),
        P("ctx"),
        P("ctx"),
    )
    out_specs = (P("ctx", "head"), P(("ctx", "head"), None), P(("ctx", "head"), None))
    return jax.shard_map(shards, mesh=mesh, in_specs=in_specs, out_specs=out_specs, check_vma=False)
```

profile of v0, /device:TPU:0, one launch (start us, length us, event | category | flops | bytes accessed | tf_op | source)
XLA Modules:
  0.0 84.9 jit_solution(3521006883890592244)
XLA Ops:
  0.6 1.5 %copy.214 = bf16[8,2,8,256]{3,2,0,1:T(8,128)(2,1)} copy(bf16[8,2,8,256]{3,2,1,0:T(8,128)(2,1)} %bitcast.208) | data formatting | bytes 131072 | tf_op jit(solution)/shard_map/all_to_all | solution.py:80
  2.2 4.2 %all-to-all-start = ((bf16[64,2,256]{2,0,1:T(8,128)(2,1)}), bf16[64,2,256]{2,0,1:T(8,128)(2,1)S(1)}, u32[]{:S(2)}, u32[]{:S(2)}) async-start(bf16[64,2,256]{2,0,1:T(8,128)(2,1)} %bitcast.137), calls=%async_computation | async-start | bytes 131072 | tf_op jit(solution)/shard_map/all_to_all | solution.py:80
  7.6 1.0 %multiply_bitcast_fusion = f32[16,8,8,128]{3,1,2,0:T(8,128)S(1)} fusion(bf16[128,1024]{1,0:T(8,128)(2,1)} %param.13, bf16[128,1024]{1,0:T(8,128)(2,1)S(1)} %copy-done), kind=kLoop, calls=%fused_computation.27 | loop fusion | flops 393216 | bytes 1048576
  10.7 3.3 %all-to-all-start.1 = ((bf16[64,2,256]{2,0,1:T(8,128)(2,1)}), bf16[64,2,256]{2,0,1:T(8,128)(2,1)S(1)}, u32[]{:S(2)}, u32[]{:S(2)}) async-start(bf16[64,2,256]{2,0,1:T(8,128)(2,1)} %bitcast.136), calls=%async_computation.1 | async-start | bytes 131072 | tf_op jit(solution)/shard_map/all_to_all | solution.py:81
  14.1 12.9 %all-reduce = s32[16]{0:T(128)S(1)} all-reduce(s32[16]{0:T(128)S(1)} %slice_dynamic-update-slice_fusion), channel_id=1, replica_groups=mesh['ctx'=16,'head'=2] {'ctx'}, use_global_device_ids=true, to_apply=%add | all-reduce | flops 16 | bytes 128
  30.8 32.3 %while.23 = (s32[]{:T(128)}, f32[128,1024]{0,1:T(8,128)S(1)}, bf16[128,256]{0,1:T(8,128)(2,1)S(1)}, bf16[128,256]{0,1:T(8,128)(2,1)S(1)}, f32[128,256]{0,1:T(8,1...) while((s32[]{:T(128)}, f32[128,1024]{0,1:T(8,128)S(1)}, ...), condition=%wide.region_2.3_spmd, body=%wide.region_1.2_spmd.sunk | while | flops 169066640 | bytes 8628740 | solution.py:112
  32.2 3.6 %collective-permute-start.2 = (f32[128,256]{0,1:T(8,128)S(1)}, f32[128,256]{0,1:T(8,128)S(1)}, u32[]{:S(2)}, u32[]{:S(2)}) collective-permute-start(f32[128,256]{0,1:T(8,128)S(1)} %get-tuple-element.559), channel_id=1, source_target_pairs={{0,8},{2,10},{4,12},{6,14},{8,16},{10,18},{12,20},{14,22},{16,24},... | collective-permute-start | bytes 393224 | tf_op jit(solution)/shard_map/while/body/eval_jaxpr/ppermute | solution.py:12
  37.2 1.2 %collective-permute-done = bf16[128,256]{0,1:T(8,128)(2,1)S(1)} collective-permute-done((bf16[128,256]{0,1:T(8,128)(2,1)S(1)}, bf16[128,256]{0,1:T(8,128)(2,1)S(1)}, u32[]{:S(2)}, u32[]{:S(2)}) %collective-permute-start) | collective-permute-done | bytes 65568 | tf_op jit(solution)/shard_map/while/body/eval_jaxpr/ppermute | solution.py:12
  39.8 1.4 %collective-permute-done.2 = f32[128,256]{0,1:T(8,128)S(1)} collective-permute-done((f32[128,256]{0,1:T(8,128)S(1)}, f32[128,256]{0,1:T(8,128)S(1)}, u32[]{:S(2)}, u32[]{:S(2)}) %collective-permute-start.2) | collective-permute-done | bytes 131104 | tf_op jit(solution)/shard_map/while/body/eval_jaxpr/ppermute | solution.py:12
  41.2 1.2 %collective-permute-start = (bf16[128,256]{0,1:T(8,128)(2,1)S(1)}, bf16[128,256]{0,1:T(8,128)(2,1)S(1)}, u32[]{:S(2)}, u32[]{:S(2)}) collective-permute-start(bf16[128,256]{0,1:T(8,128)(2,1)S(1)} %get-tuple-element.557), channel_id=1, source_target_pairs={{0,8},{2,10},{4,12},{6,14},{8,16},{10,18},{12,20},{14,22},{16,24},... | collective-permute-start | bytes 196616 | tf_op jit(solution)/shard_map/while/body/eval_jaxpr/ppermute | solution.py:12
  42.4 1.3 %collective-permute-start.3 = (f32[128,256]{0,1:T(8,128)S(1)}, f32[128,256]{0,1:T(8,128)S(1)}, u32[]{:S(2)}, u32[]{:S(2)}) collective-permute-start(f32[128,256]{0,1:T(8,128)S(1)} %get-tuple-element.560), channel_id=1, source_target_pairs={{0,8},{2,10},{4,12},{6,14},{8,16},{10,18},{12,20},{14,22},{16,24},... | collective-permute-start | bytes 393224 | tf_op jit(solution)/shard_map/while/body/eval_jaxpr/ppermute | solution.py:12
  43.7 2.5 %collective-permute-start.2 = (f32[128,256]{0,1:T(8,128)S(1)}, f32[128,256]{0,1:T(8,128)S(1)}, u32[]{:S(2)}, u32[]{:S(2)}) collective-permute-start(f32[128,256]{0,1:T(8,128)S(1)} %get-tuple-element.559), channel_id=1, source_target_pairs={{0,8},{2,10},{4,12},{6,14},{8,16},{10,18},{12,20},{14,22},{16,24},... | collective-permute-start | bytes 393224 | tf_op jit(solution)/shard_map/while/body/eval_jaxpr/ppermute | solution.py:12
  49.4 1.4 %collective-permute-done.2 = f32[128,256]{0,1:T(8,128)S(1)} collective-permute-done((f32[128,256]{0,1:T(8,128)S(1)}, f32[128,256]{0,1:T(8,128)S(1)}, u32[]{:S(2)}, u32[]{:S(2)}) %collective-permute-start.2) | collective-permute-done | bytes 131104 | tf_op jit(solution)/shard_map/while/body/eval_jaxpr/ppermute | solution.py:12
  50.8 1.5 %collective-permute-start.1 = (bf16[128,256]{0,1:T(8,128)(2,1)S(1)}, bf16[128,256]{0,1:T(8,128)(2,1)S(1)}, u32[]{:S(2)}, u32[]{:S(2)}) collective-permute-start(bf16[128,256]{0,1:T(8,128)(2,1)S(1)} %get-tuple-element.558), channel_id=1, source_target_pairs={{0,8},{2,10},{4,12},{6,14},{8,16},{10,18},{12,20},{14,22},{16,24},... | collective-permute-start | bytes 196616 | tf_op jit(solution)/shard_map/while/body/eval_jaxpr/ppermute | solution.py:12
  52.3 1.2 %collective-permute-start = (bf16[128,256]{0,1:T(8,128)(2,1)S(1)}, bf16[128,256]{0,1:T(8,128)(2,1)S(1)}, u32[]{:S(2)}, u32[]{:S(2)}) collective-permute-start(bf16[128,256]{0,1:T(8,128)(2,1)S(1)} %get-tuple-element.557), channel_id=1, source_target_pairs={{0,8},{2,10},{4,12},{6,14},{8,16},{10,18},{12,20},{14,22},{16,24},... | collective-permute-start | bytes 196616 | tf_op jit(solution)/shard_map/while/body/eval_jaxpr/ppermute | solution.py:12
  54.3 1.5 %collective-permute-start.2 = (f32[128,256]{0,1:T(8,128)S(1)}, f32[128,256]{0,1:T(8,128)S(1)}, u32[]{:S(2)}, u32[]{:S(2)}) collective-permute-start(f32[128,256]{0,1:T(8,128)S(1)} %get-tuple-element.559), channel_id=1, source_target_pairs={{0,8},{2,10},{4,12},{6,14},{8,16},{10,18},{12,20},{14,22},{16,24},... | collective-permute-start | bytes 393224 | tf_op jit(solution)/shard_map/while/body/eval_jaxpr/ppermute | solution.py:12
  57.2 1.2 %collective-permute-done = bf16[128,256]{0,1:T(8,128)(2,1)S(1)} collective-permute-done((bf16[128,256]{0,1:T(8,128)(2,1)S(1)}, bf16[128,256]{0,1:T(8,128)(2,1)S(1)}, u32[]{:S(2)}, u32[]{:S(2)}) %collective-permute-start) | collective-permute-done | bytes 65568 | tf_op jit(solution)/shard_map/while/body/eval_jaxpr/ppermute | solution.py:12
  60.5 2.6 %collective-permute-done.2 = f32[128,256]{0,1:T(8,128)S(1)} collective-permute-done((f32[128,256]{0,1:T(8,128)S(1)}, f32[128,256]{0,1:T(8,128)S(1)}, u32[]{:S(2)}, u32[]{:S(2)}) %collective-permute-start.2) | collective-permute-done | bytes 131104 | tf_op jit(solution)/shard_map/while/body/eval_jaxpr/ppermute | solution.py:12
  63.9 5.5 %collective-permute-done.4 = bf16[128,256]{1,0:T(8,128)(2,1)} collective-permute-done((bf16[128,256]{1,0:T(8,128)(2,1)S(1)}, bf16[128,256]{1,0:T(8,128)(2,1)}, u32[]{:S(2)}, u32[]{:S(2)}) %collective-permute-start.4) | collective-permute-done | bytes 65568 | tf_op jit(solution)/shard_map/ppermute | solution.py:12
  69.4 3.3 %all-to-all-start.2 = ((bf16[2,64,256]{2,1,0:T(8,128)(2,1)}), bf16[2,64,256]{2,1,0:T(8,128)(2,1)S(1)}, u32[]{:S(2)}, u32[]{:S(2)}) async-start(bf16[2,64,256]{2,1,0:T(8,128)(2,1)} %bitcast.46), calls=%async_computation.2 | async-start | bytes 131072 | tf_op jit(solution)/shard_map/all_to_all | solution.py:120
  72.7 4.1 %all-to-all-done.2 = bf16[2,64,256]{2,1,0:T(8,128)(2,1)S(1)} async-done(((bf16[2,64,256]{2,1,0:T(8,128)(2,1)}), bf16[2,64,256]{2,1,0:T(8,128)(2,1)S(1)}, u32[]{:S(2)}, u32[]{:S(2)}) %all-to-all-start.2) | async-done | bytes 65568 | tf_op jit(solution)/shard_map/all_to_all | solution.py:120
  76.8 3.3 %all-to-all-start.3 = ((bf16[2,64,256]{2,1,0:T(8,128)(2,1)}), bf16[2,64,256]{2,1,0:T(8,128)(2,1)S(1)}, u32[]{:S(2)}, u32[]{:S(2)}) async-start(bf16[2,64,256]{2,1,0:T(8,128)(2,1)} %bitcast.48), calls=%async_computation.3 | async-start | bytes 131072 | tf_op jit(solution)/shard_map/all_to_all | solution.py:123
  80.1 0.8 copy.169
  81.6 2.6 %all-to-all-done.3 = bf16[2,64,256]{2,1,0:T(8,128)(2,1)S(1)} async-done(((bf16[2,64,256]{2,1,0:T(8,128)(2,1)}), bf16[2,64,256]{2,1,0:T(8,128)(2,1)S(1)}, u32[]{:S(2)}, u32[]{:S(2)}) %all-to-all-start.3) | async-done | bytes 65568 | tf_op jit(solution)/shard_map/all_to_all | solution.py:123
  (95 shorter events, 20.6 us)
Async XLA Ops:
  0.6 7.0 %copy-start = (bf16[128,1024]{1,0:T(8,128)(2,1)S(1)}, bf16[128,1024]{1,0:T(8,128)(2,1)}, u32[]{:S(2)}) copy-start(bf16[128,1024]{1,0:T(8,128)(2,1)} %param.14) | copy-start | bytes 786436
  2.2 8.6 %all-to-all-start = ((bf16[64,2,256]{2,0,1:T(8,128)(2,1)}), bf16[64,2,256]{2,0,1:T(8,128)(2,1)S(1)}, u32[]{:S(2)}, u32[]{:S(2)}) async-start(bf16[64,2,256]{2,0,1:T(8,128)(2,1)} %bitcast.137), calls=%async_computation | async-start | bytes 131072 | tf_op jit(solution)/shard_map/all_to_all | solution.py:80
  7.6 2.5 %copy-start.3 = (bf16[64,512]{1,0:T(8,128)(2,1)S(1)}, bf16[64,512]{1,0:T(8,128)(2,1)}, u32[]{:S(2)}) copy-start(bf16[64,512]{1,0:T(8,128)(2,1)} %param.12) | copy-start | bytes 196612
  8.7 0.7 copy-start.4
  9.3 0.8 copy-start.5
  10.7 17.9 %all-to-all-start.1 = ((bf16[64,2,256]{2,0,1:T(8,128)(2,1)}), bf16[64,2,256]{2,0,1:T(8,128)(2,1)S(1)}, u32[]{:S(2)}, u32[]{:S(2)}) async-start(bf16[64,2,256]{2,0,1:T(8,128)(2,1)} %bitcast.136), calls=%async_computation.1 | async-start | bytes 131072 | tf_op jit(solution)/shard_map/all_to_all | solution.py:81
  27.0 0.9 %copy-start.1 = (bf16[128,1024]{1,0:T(8,128)(2,1)S(1)}, bf16[128,1024]{1,0:T(8,128)(2,1)}, u32[]{:S(2)}) copy-start(bf16[128,1024]{1,0:T(8,128)(2,1)} %param.10) | copy-start | bytes 786436
  28.6 0.7 copy-start.2
  30.8 8.0 %collective-permute-start.1 = (bf16[128,256]{0,1:T(8,128)(2,1)S(1)}, bf16[128,256]{0,1:T(8,128)(2,1)S(1)}, u32[]{:S(2)}, u32[]{:S(2)}) collective-permute-start(bf16[128,256]{0,1:T(8,128)(2,1)S(1)} %get-tuple-element.558), channel_id=1, source_target_pairs={{0,8},{2,10},{4,12},{6,14},{8,16},{10,18},{12,20},{14,22},{16,24},... | collective-permute-start | bytes 196616 | tf_op jit(solution)/shard_map/while/body/eval_jaxpr/ppermute | solution.py:12
  31.3 7.0 %collective-permute-start = (bf16[128,256]{0,1:T(8,128)(2,1)S(1)}, bf16[128,256]{0,1:T(8,128)(2,1)S(1)}, u32[]{:S(2)}, u32[]{:S(2)}) collective-permute-start(bf16[128,256]{0,1:T(8,128)(2,1)S(1)} %get-tuple-element.557), channel_id=1, source_target_pairs={{0,8},{2,10},{4,12},{6,14},{8,16},{10,18},{12,20},{14,22},{16,24},... | collective-permute-start | bytes 196616 | tf_op jit(solution)/shard_map/while/body/eval_jaxpr/ppermute | solution.py:12
  31.8 8.0 %collective-permute-start.3 = (f32[128,256]{0,1:T(8,128)S(1)}, f32[128,256]{0,1:T(8,128)S(1)}, u32[]{:S(2)}, u32[]{:S(2)}) collective-permute-start(f32[128,256]{0,1:T(8,128)S(1)} %get-tuple-element.560), channel_id=1, source_target_pairs={{0,8},{2,10},{4,12},{6,14},{8,16},{10,18},{12,20},{14,22},{16,24},... | collective-permute-start | bytes 393224 | tf_op jit(solution)/shard_map/while/body/eval_jaxpr/ppermute | solution.py:12
  32.2 8.9 %collective-permute-start.2 = (f32[128,256]{0,1:T(8,128)S(1)}, f32[128,256]{0,1:T(8,128)S(1)}, u32[]{:S(2)}, u32[]{:S(2)}) collective-permute-start(f32[128,256]{0,1:T(8,128)S(1)} %get-tuple-element.559), channel_id=1, source_target_pairs={{0,8},{2,10},{4,12},{6,14},{8,16},{10,18},{12,20},{14,22},{16,24},... | collective-permute-start | bytes 393224 | tf_op jit(solution)/shard_map/while/body/eval_jaxpr/ppermute | solution.py:12
  41.2 7.4 %collective-permute-start.1 = (bf16[128,256]{0,1:T(8,128)(2,1)S(1)}, bf16[128,256]{0,1:T(8,128)(2,1)S(1)}, u32[]{:S(2)}, u32[]{:S(2)}) collective-permute-start(bf16[128,256]{0,1:T(8,128)(2,1)S(1)} %get-tuple-element.558), channel_id=1, source_target_pairs={{0,8},{2,10},{4,12},{6,14},{8,16},{10,18},{12,20},{14,22},{16,24},... | collective-permute-start | bytes 196616 | tf_op jit(solution)/shard_map/while/body/eval_jaxpr/ppermute | solution.py:12
  41.2 6.8 %collective-permute-start = (bf16[128,256]{0,1:T(8,128)(2,1)S(1)}, bf16[128,256]{0,1:T(8,128)(2,1)S(1)}, u32[]{:S(2)}, u32[]{:S(2)}) collective-permute-start(bf16[128,256]{0,1:T(8,128)(2,1)S(1)} %get-tuple-element.557), channel_id=1, source_target_pairs={{0,8},{2,10},{4,12},{6,14},{8,16},{10,18},{12,20},{14,22},{16,24},... | collective-permute-start | bytes 196616 | tf_op jit(solution)/shard_map/while/body/eval_jaxpr/ppermute | solution.py:12
  42.4 7.0 %collective-permute-start.3 = (f32[128,256]{0,1:T(8,128)S(1)}, f32[128,256]{0,1:T(8,128)S(1)}, u32[]{:S(2)}, u32[]{:S(2)}) collective-permute-start(f32[128,256]{0,1:T(8,128)S(1)} %get-tuple-element.560), channel_id=1, source_target_pairs={{0,8},{2,10},{4,12},{6,14},{8,16},{10,18},{12,20},{14,22},{16,24},... | collective-permute-start | bytes 393224 | tf_op jit(solution)/shard_map/while/body/eval_jaxpr/ppermute | solution.py:12
  43.7 7.1 %collective-permute-start.2 = (f32[128,256]{0,1:T(8,128)S(1)}, f32[128,256]{0,1:T(8,128)S(1)}, u32[]{:S(2)}, u32[]{:S(2)}) collective-permute-start(f32[128,256]{0,1:T(8,128)S(1)} %get-tuple-element.559), channel_id=1, source_target_pairs={{0,8},{2,10},{4,12},{6,14},{8,16},{10,18},{12,20},{14,22},{16,24},... | collective-permute-start | bytes 393224 | tf_op jit(solution)/shard_map/while/body/eval_jaxpr/ppermute | solution.py:12
  50.8 8.1 %collective-permute-start.1 = (bf16[128,256]{0,1:T(8,128)(2,1)S(1)}, bf16[128,256]{0,1:T(8,128)(2,1)S(1)}, u32[]{:S(2)}, u32[]{:S(2)}) collective-permute-start(bf16[128,256]{0,1:T(8,128)(2,1)S(1)} %get-tuple-element.558), channel_id=1, source_target_pairs={{0,8},{2,10},{4,12},{6,14},{8,16},{10,18},{12,20},{14,22},{16,24},... | collective-permute-start | bytes 196616 | tf_op jit(solution)/shard_map/while/body/eval_jaxpr/ppermute | solution.py:12
  52.3 6.1 %collective-permute-start = (bf16[128,256]{0,1:T(8,128)(2,1)S(1)}, bf16[128,256]{0,1:T(8,128)(2,1)S(1)}, u32[]{:S(2)}, u32[]{:S(2)}) collective-permute-start(bf16[128,256]{0,1:T(8,128)(2,1)S(1)} %get-tuple-element.557), channel_id=1, source_target_pairs={{0,8},{2,10},{4,12},{6,14},{8,16},{10,18},{12,20},{14,22},{16,24},... | collective-permute-start | bytes 196616 | tf_op jit(solution)/shard_map/while/body/eval_jaxpr/ppermute | solution.py:12
  53.5 6.9 %collective-permute-start.3 = (f32[128,256]{0,1:T(8,128)S(1)}, f32[128,256]{0,1:T(8,128)S(1)}, u32[]{:S(2)}, u32[]{:S(2)}) collective-permute-start(f32[128,256]{0,1:T(8,128)S(1)} %get-tuple-element.560), channel_id=1, source_target_pairs={{0,8},{2,10},{4,12},{6,14},{8,16},{10,18},{12,20},{14,22},{16,24},... | collective-permute-start | bytes 393224 | tf_op jit(solution)/shard_map/while/body/eval_jaxpr/ppermute | solution.py:12
  54.3 8.7 %collective-permute-start.2 = (f32[128,256]{0,1:T(8,128)S(1)}, f32[128,256]{0,1:T(8,128)S(1)}, u32[]{:S(2)}, u32[]{:S(2)}) collective-permute-start(f32[128,256]{0,1:T(8,128)S(1)} %get-tuple-element.559), channel_id=1, source_target_pairs={{0,8},{2,10},{4,12},{6,14},{8,16},{10,18},{12,20},{14,22},{16,24},... | collective-permute-start | bytes 393224 | tf_op jit(solution)/shard_map/while/body/eval_jaxpr/ppermute | solution.py:12
  63.2 6.2 %collective-permute-start.4 = (bf16[128,256]{1,0:T(8,128)(2,1)S(1)}, bf16[128,256]{1,0:T(8,128)(2,1)}, u32[]{:S(2)}, u32[]{:S(2)}) collective-permute-start(bf16[128,256]{1,0:T(8,128)(2,1)S(1)} %copy.170), channel_id=1, source_target_pairs={{0,8},{2,10},{4,12},{6,14},{8,16},{10,18},{12,20},{14,22},{16,24},... | collective-permute-start | bytes 196616 | tf_op jit(solution)/shard_map/ppermute | solution.py:12
  63.4 9.4 %collective-permute-start.5 = (bf16[128,256]{1,0:T(8,128)(2,1)S(1)}, bf16[128,256]{1,0:T(8,128)(2,1)}, u32[]{:S(2)}, u32[]{:S(2)}) collective-permute-start(bf16[128,256]{1,0:T(8,128)(2,1)S(1)} %copy.172), channel_id=1, source_target_pairs={{0,8},{2,10},{4,12},{6,14},{8,16},{10,18},{12,20},{14,22},{16,24},... | collective-permute-start | bytes 196616 | tf_op jit(solution)/shard_map/ppermute | solution.py:12
  69.4 7.4 %all-to-all-start.2 = ((bf16[2,64,256]{2,1,0:T(8,128)(2,1)}), bf16[2,64,256]{2,1,0:T(8,128)(2,1)S(1)}, u32[]{:S(2)}, u32[]{:S(2)}) async-start(bf16[2,64,256]{2,1,0:T(8,128)(2,1)} %bitcast.46), calls=%async_computation.2 | async-start | bytes 131072 | tf_op jit(solution)/shard_map/all_to_all | solution.py:120
  76.8 7.4 %all-to-all-start.3 = ((bf16[2,64,256]{2,1,0:T(8,128)(2,1)}), bf16[2,64,256]{2,1,0:T(8,128)(2,1)S(1)}, u32[]{:S(2)}, u32[]{:S(2)}) async-start(bf16[2,64,256]{2,1,0:T(8,128)(2,1)} %bitcast.48), calls=%async_computation.3 | async-start | bytes 131072 | tf_op jit(solution)/shard_map/all_to_all | solution.py:123
  (1 other events, 0.7 us)
where the time goes:
time: 85.6 us; the launch traced here: 84.9 us
  starting transfers between devices  29.7 us (35%)
  waiting for transfers between devices  21.2 us (25%)
  blocking collectives  12.9 us (15%)
  local copies, waits for them, and re-layouts  11.2 us (13%)
  matrix products  4.89 us (6%)
  other arithmetic  3.85 us (4%)
  between operations  0.86 us (1%)
    ppermute x14, starting transfers between devices, from_behind(): return lax.ppermute(value, axis, pairs)  15.6 us
    ppermute x14, waiting for transfers between devices, from_behind(): return lax.ppermute(value, axis, pairs)  14.5 us
    unnamed x1, blocking collectives  12.9 us
    all_to_all x1, starting transfers between devices, shards(): lax.all_to_all(key_states, 'head', split_axis=1, concat_axis=0, tiled=True)  4.21 us
    unnamed x18, local copies, waits for them, and re-layouts  4.17 us
    all_to_all x1, waiting for transfers between devices, shards(): lax.all_to_all(key_grad.astype(jnp.bfloat16), 'head', split_axis=0, conca...  4.1 us
    all_to_all x1, starting transfers between devices, shards(): lax.all_to_all(value_states, 'head', split_axis=1, concat_axis=0, tiled=T...  3.31 us
    all_to_all x1, starting transfers between devices, shards(): lax.all_to_all(key_grad.astype(jnp.bfloat16), 'head', split_axis=0, conca...  3.3 us
  transfers between devices with their start and end apart: 18, of which 10 were waited for; matrix products, arithmetic and copies ran while one was open for 16% of the time, Pallas kernels for 0%

commit v1 on v0

v1 whole, which is shorter than its diff:
```python
import functools

import jax
import jax.numpy as jnp
from jax import lax
from jax.experimental import pallas as pl
from jax.experimental.pallas import tpu as pltpu
from jax.sharding import PartitionSpec as P

HEAD_DIM = 128
QUARTERS = 4
MESH = pl.DeviceIdType.MESH


def dot(a, b, dims):
    return lax.dot_general(a, b, (dims, ((), ())), preferred_element_type=jnp.float32)


def kernel(
    members, groups,
    q_hbm, k_hbm, v_hbm, o_hbm, g_hbm, lse_ref, order_ref, pos_ref,
    dq_hbm, dk_hbm, dv_hbm,
    q_buf, o_buf, g_buf, q_tall, g_tall, k_all, v_all, order_all,
    lse_wide, dot_wide, ds_all, k_part, v_part, k_in, v_in, dq_buf, dk_buf, dv_buf,
    local_sem, send_kv, recv_kv, send_order, recv_order, send_grad, recv_grad,
):
    ctx, mine = lax.axis_index("ctx"), lax.axis_index("head")
    me, quarter = ctx // QUARTERS, lax.rem(ctx, QUARTERS)
    own = k_hbm.shape[0]
    rows = q_hbm.shape[0]
    kv_columns = k_hbm.shape[1] // groups
    kv_local = kv_columns // HEAD_DIM
    group_size = q_hbm.shape[1] // kv_columns
    wide = group_size * rows
    scale = HEAD_DIM ** (-0.5)

    def loop(low, high, body):
        if members <= 4:
            for step in range(low, high):
                body(step)
        else:
            def call(step, carry):
                body(step)
                return carry
            lax.fori_loop(low, high, call, 0)

    def device(member, head):
        return (member * QUARTERS + quarter, head)

    def member_at(step):
        return lax.rem(me + step, members)

    def head_at(step):
        return lax.rem(mine + step, groups)

    def columns(head):
        return pl.ds(pl.multiple_of(head * kv_columns, kv_columns), kv_columns)

    def half(head):
        return pl.ds(pl.multiple_of(head * own, own), own)

    def kv_copy(which, member, head, sender, sender_head):
        source = (k_hbm, v_hbm)[which]
        target = (k_all, v_all)[which]
        return pltpu.make_async_remote_copy(
            src_ref=source.at[:, columns(head)],
            dst_ref=target.at[sender, half(sender_head)],
            send_sem=send_kv.at[which, member, head],
            recv_sem=recv_kv.at[which, sender, sender_head],
            device_id=device(member, head),
            device_id_type=MESH,
        )

    def order_copy(member, sender):
        return pltpu.make_async_remote_copy(
            src_ref=order_ref,
            dst_ref=order_all.at[sender],
            send_sem=send_order.at[member],
            recv_sem=recv_order.at[sender],
            device_id=device(member, mine),
            device_id_type=MESH,
        )

    def grad_copy(which, member, head, sender, sender_head):
        source = (k_part, v_part)[which]
        target = (k_in, v_in)[which]
        return pltpu.make_async_remote_copy(
            src_ref=source.at[member, half(head)],
            dst_ref=target.at[sender, :, columns(sender_head)],
            send_sem=send_grad.at[which, member, head],
            recv_sem=recv_grad.at[which, sender, sender_head],
            device_id=device(member, head),
            device_id_type=MESH,
        )

    loads = [
        pltpu.make_async_copy(k_hbm.at[:, columns(mine)], k_all.at[me, half(mine)], local_sem.at[0]),
        pltpu.make_async_copy(v_hbm.at[:, columns(mine)], v_all.at[me, half(mine)], local_sem.at[1]),
        pltpu.make_async_copy(q_hbm, q_buf, local_sem.at[2]),
        pltpu.make_async_copy(o_hbm, o_buf, local_sem.at[3]),
        pltpu.make_async_copy(g_hbm, g_buf, local_sem.at[4]),
    ]
    for load in loads:
        load.start()

    barrier = pltpu.get_barrier_semaphore()

    def greet(step):
        for head_step in range(groups):
            def signal():
                pl.semaphore_signal(
                    barrier, inc=1, device_id=device(member_at(step), head_at(head_step)),
                    device_id_type=MESH,
                )
            signal()

    for head_step in range(1, groups):
        pl.semaphore_signal(
            barrier, inc=1, device_id=device(me, head_at(head_step)), device_id_type=MESH
        )
    loop(1, members, greet)
    pl.semaphore_wait(barrier, members * groups - 1)

    def push(step):
        member = member_at(step)
        order_copy(member, me).start()
        for head_step in range(groups):
            for which in range(2):
                kv_copy(which, member, head_at(head_step), me, mine).start()

    loop(1, members, push)
    for head_step in range(1, groups):
        for which in range(2):
            kv_copy(which, me, head_at(head_step), me, mine).start()

    for load in loads:
        load.wait()
    for head in range(group_size * kv_local):
        kv_head, place = head // group_size, head % group_size
        spot = slice(place * rows, (place + 1) * rows)
        lanes = slice(head * HEAD_DIM, (head + 1) * HEAD_DIM)
        grad = g_buf[:, lanes]
        q_tall[kv_head, spot, :] = q_buf[:, lanes]
        g_tall[kv_head, spot, :] = grad
        product = grad.astype(jnp.float32) * o_buf[:, lanes].astype(jnp.float32)
        dot_wide[kv_head : kv_head + 1, spot] = jnp.sum(product.T, axis=0, keepdims=True)
        lse_wide[kv_head : kv_head + 1, spot] = lse_ref[head : head + 1, :]
    order_all[me] = order_ref[...]

    last = order_ref[...]
    first = last - pos_ref[...]
    lane = lax.broadcasted_iota(jnp.int32, (1, rows), 1)
    place_in_block = lax.broadcasted_iota(jnp.int32, (rows, rows), 0)

    def block(member):
        start = order_all[member] - lane
        visible = (place_in_block <= last - start) & (place_in_block >= first - start)
        visible = jnp.concatenate([visible.astype(jnp.float32)] * group_size, axis=1) > 0.5
        for kv_head in range(kv_local):
            lanes = slice(kv_head * HEAD_DIM, (kv_head + 1) * HEAD_DIM)
            keys, values = k_all[member, :, lanes], v_all[member, :, lanes]
            queries, grads = q_tall[kv_head], g_tall[kv_head]
            scores = dot(keys, queries, ((1,), (1,))) * scale
            prob_grad = dot(values, grads, ((1,), (1,)))
            probs = jnp.where(visible, jnp.exp(scores - lse_wide[kv_head : kv_head + 1, :]), 0.0)
            score_grad = (
                probs * (prob_grad - dot_wide[kv_head : kv_head + 1, :]) * scale
            ).astype(jnp.bfloat16)
            ds_all[kv_head, pl.ds(pl.multiple_of(member * rows, rows), rows), :] = score_grad
            v_part[member, :, lanes] = dot(
                probs.astype(jnp.bfloat16), grads, ((1,), (0,))
            ).astype(jnp.bfloat16)
            k_part[member, :, lanes] = dot(score_grad, queries, ((1,), (0,))).astype(jnp.bfloat16)

    for head_step in range(1, groups):
        for which in range(2):
            kv_copy(which, me, head_at(head_step), me, head_at(head_step)).wait_recv()
    block(me)
    k_in[me, :, columns(mine)] = k_part[me, half(mine), :]
    v_in[me, :, columns(mine)] = v_part[me, half(mine), :]
    for head_step in range(1, groups):
        for which in range(2):
            grad_copy(which, me, head_at(head_step), me, mine).start()

    def visit(step):
        member = member_at(step)
        order_copy(member, member).wait_recv()
        for head_step in range(groups):
            for which in range(2):
                kv_copy(which, member, head_at(head_step), member, head_at(head_step)).wait_recv()
        block(member)
        for head_step in range(groups):
            for which in range(2):
                grad_copy(which, member, head_at(head_step), me, mine).start()

    loop(1, members, visit)

    keys_tall = k_all[...].reshape(members * rows, kv_columns)
    for kv_head in range(kv_local):
        keys = keys_tall[:, kv_head * HEAD_DIM : (kv_head + 1) * HEAD_DIM]
        update = dot(ds_all[kv_head], keys, ((0,), (0,))).astype(jnp.bfloat16)
        for place in range(group_size):
            head = kv_head * group_size + place
            dq_buf[:, head * HEAD_DIM : (head + 1) * HEAD_DIM] = update[
                place * rows : (place + 1) * rows, :
            ]
    dq_out = pltpu.make_async_copy(dq_buf, dq_hbm, local_sem.at[5])
    dq_out.start()

    def sent(step):
        member = member_at(step)
        order_copy(member, me).wait_send()
        for head_step in range(groups):
            for which in range(2):
                kv_copy(which, member, head_at(head_step), me, mine).wait_send()
                grad_copy(which, member, head_at(head_step), me, mine).wait_send()
                grad_copy(which, member, head_at(head_step), member, head_at(head_step)).wait_recv()

    for head_step in range(1, groups):
        for which in range(2):
            kv_copy(which, me, head_at(head_step), me, mine).wait_send()
            grad_copy(which, me, head_at(head_step), me, mine).wait_send()
            grad_copy(which, me, head_at(head_step), me, head_at(head_step)).wait_recv()
    loop(1, members, sent)

    outs = []
    for which, (inbox, buf, out) in enumerate(((k_in, dk_buf, dk_hbm), (v_in, dv_buf, dv_hbm))):
        buf[...] = jnp.sum(inbox[...].astype(jnp.float32), axis=0).astype(jnp.bfloat16)
        copy = pltpu.make_async_copy(buf, out, local_sem.at[6 + which])
        copy.start()
        outs.append(copy)
    dq_out.wait()
    for copy in outs:
        copy.wait()


def shards(
    queries, key_states, value_states, attn_out, grad_out, log_sum_exp, token_order, position
):
    members = lax.axis_size("ctx") // QUARTERS
    groups = lax.axis_size("head")
    rows, head_columns = queries.shape
    own, kv_total = key_states.shape
    kv_columns = kv_total // groups
    kv_local = kv_columns // HEAD_DIM
    wide = rows * (head_columns // kv_columns)
    anywhere = pl.BlockSpec(memory_space=pl.ANY)
    vmem = pl.BlockSpec(memory_space=pltpu.VMEM)
    bf16, f32 = jnp.bfloat16, jnp.float32
    dma = pltpu.SemaphoreType.DMA
    return pl.pallas_call(
        functools.partial(kernel, members, groups),
        out_shape=(
            jax.ShapeDtypeStruct(queries.shape, bf16),
            jax.ShapeDtypeStruct(key_states.shape, bf16),
            jax.ShapeDtypeStruct(value_states.shape, bf16),
        ),
        in_specs=[anywhere] * 5 + [vmem] * 3,
        out_specs=(anywhere,) * 3,
        scratch_shapes=[
            pltpu.VMEM((rows, head_columns), bf16),
            pltpu.VMEM((rows, head_columns), bf16),
            pltpu.VMEM((rows, head_columns), bf16),
            pltpu.VMEM((kv_local, wide, HEAD_DIM), bf16),
            pltpu.VMEM((kv_local, wide, HEAD_DIM), bf16),
            pltpu.VMEM((members, rows, kv_columns), bf16),
            pltpu.VMEM((members, rows, kv_columns), bf16),
            pltpu.VMEM((members, 1, rows), jnp.int32),
            pltpu.VMEM((kv_local, wide), f32),
            pltpu.VMEM((kv_local, wide), f32),
            pltpu.VMEM((kv_local, members * rows, wide), bf16),
            pltpu.VMEM((members, rows, kv_columns), bf16),
            pltpu.VMEM((members, rows, kv_columns), bf16),
            pltpu.VMEM((members, own, kv_total), bf16),
            pltpu.VMEM((members, own, kv_total), bf16),
            pltpu.VMEM((rows, head_columns), bf16),
            pltpu.VMEM((own, kv_total), bf16),
            pltpu.VMEM((own, kv_total), bf16),
            dma((8,)),
            dma((2, members, groups)),
            dma((2, members, groups)),
            dma((members,)),
            dma((members,)),
            dma((2, members, groups)),
            dma((2, members, groups)),
        ],
        compiler_params=pltpu.CompilerParams(
            collective_id=0, has_side_effects=True, vmem_limit_bytes=48 * 1024 * 1024
        ),
    )(
        queries, key_states, value_states, attn_out, grad_out, log_sum_exp,
        token_order.reshape(1, rows), position.reshape(1, rows),
    )


def solution(mesh):
    in_specs = (
        P("ctx", "head"),
        P(("ctx", "head"), None),
        P(("ctx", "head"), None),
        P("ctx", "head"),
        P("ctx", "head"),
        P("head", "ctx"),
        P("ctx"),
        P("ctx"),
    )
    out_specs = (P("ctx", "head"), P(("ctx", "head"), None), P(("ctx", "head"), None))
    return jax.shard_map(shards, mesh=mesh, in_specs=in_specs, out_specs=out_specs, check_vma=False)
```

time: 85.6 us -> 39.3 us (0.46)
  the two profiles are of different devices: /device:TPU:0 before, /device:TPU:25 now
where the time goes in v1:
time: 39.3 us; the launch traced here: 38.9 us
  Pallas kernels  30.4 us (77%)
  local copies, waits for them, and re-layouts  7.83 us (20%)
  between operations  0.67 us (2%)
    pallas_call x1, Pallas kernels, shards(): pl.pallas_call(functools.partial(kernel, members, groups), out_shape=(jax...  30.4 us
    unnamed x19, local copies, waits for them, and re-layouts  7.83 us

profile of v1, /device:TPU:25, one launch (start us, length us, event | category | flops | bytes accessed | tf_op | source)
XLA Modules:
  0.0 38.9 jit_solution(5529408046711378445)
XLA Ops:
  0.6 0.0 copy-start.6
  0.6 0.0 copy-start.7
  0.7 0.6 %copy-done.6 = s32[128]{0:T(128)S(1)} copy-done((s32[128]{0:T(128)S(1)}, s32[128]{0:T(128)}, u32[]{:S(2)}) %copy-start.6) | copy-done | bytes 536
  1.3 0.0 copy-done.7
  1.3 0.0 copy-start
  1.3 0.9 %copy-done = bf16[128,1024]{1,0:T(8,128)(2,1)S(1)} copy-done((bf16[128,1024]{1,0:T(8,128)(2,1)S(1)}, bf16[128,1024]{1,0:T(8,128)(2,1)}, u32[]{:S(2)}) %copy-start) | copy-done | bytes 262168
  2.3 0.0 copy-start.1
  2.3 0.9 %copy-done.1 = bf16[128,1024]{1,0:T(8,128)(2,1)S(1)} copy-done((bf16[128,1024]{1,0:T(8,128)(2,1)S(1)}, bf16[128,1024]{1,0:T(8,128)(2,1)}, u32[]{:S(2)}) %copy-start.1) | copy-done | bytes 262168
  3.2 0.0 copy-start.2
  3.2 0.9 %copy-done.2 = bf16[128,1024]{1,0:T(8,128)(2,1)S(1)} copy-done((bf16[128,1024]{1,0:T(8,128)(2,1)S(1)}, bf16[128,1024]{1,0:T(8,128)(2,1)}, u32[]{:S(2)}) %copy-start.2) | copy-done | bytes 262168
  4.2 0.0 copy-start.3
  4.2 0.8 %copy-done.3 = bf16[64,512]{1,0:T(8,128)(2,1)S(1)} copy-done((bf16[64,512]{1,0:T(8,128)(2,1)S(1)}, bf16[64,512]{1,0:T(8,128)(2,1)}, u32[]{:S(2)}) %copy-start.3) | copy-done | bytes 65560
  5.0 0.0 copy-start.4
  5.0 0.8 %copy-done.4 = bf16[64,512]{1,0:T(8,128)(2,1)S(1)} copy-done((bf16[64,512]{1,0:T(8,128)(2,1)S(1)}, bf16[64,512]{1,0:T(8,128)(2,1)}, u32[]{:S(2)}) %copy-start.4) | copy-done | bytes 65560
  5.8 0.0 copy-start.5
  5.8 0.7 %copy-done.5 = f32[8,128]{1,0:T(8,128)S(1)} copy-done((f32[8,128]{1,0:T(8,128)S(1)}, f32[8,128]{1,0:T(8,128)}, u32[]{:S(2)}) %copy-start.5) | copy-done | bytes 4120
  6.5 30.4 %shard_map.103 = (bf16[128,1024]{1,0:T(8,128)(2,1)S(1)}, bf16[64,512]{1,0:T(8,128)(2,1)S(1)}, bf16[64,512]{1,0:T(8,128)(2,1)S(1)}) custom-call(bf16[128,1024]{1,0:T(8,128)(2,1)S(1)} %copy-done, bf16[64,512]{1,0:T(8,128)(2,1)S(1)} %copy-done.3, bf16[64,512]{1,0:T(8,128)(2,1)S(1)} %copy-done.4, bf16[128,1024]{1,0:T(8,128)(2,1)S(1)} %copy-done.1, ...), custom_call_target="tpu_custom_call" | custom-call | tf_op jit(solution)/shard_map/pallas_call | solution.py:251
  36.9 0.7 %copy.14 = bf16[128,1024]{1,0:T(8,128)(2,1)} copy(bf16[128,1024]{1,0:T(8,128)(2,1)S(1)} %get-tuple-element.6) | data formatting | bytes 524288
  37.7 0.6 %copy.15 = bf16[64,512]{1,0:T(8,128)(2,1)} copy(bf16[64,512]{1,0:T(8,128)(2,1)S(1)} %get-tuple-element.7) | data formatting | bytes 131072
  38.3 0.6 %copy.16 = bf16[64,512]{1,0:T(8,128)(2,1)} copy(bf16[64,512]{1,0:T(8,128)(2,1)S(1)} %get-tuple-element.8) | data formatting | bytes 131072
Async XLA Ops:
  0.6 0.7 %copy-start.6 = (s32[128]{0:T(128)S(1)}, s32[128]{0:T(128)}, u32[]{:S(2)}) copy-start(s32[128]{0:T(128)} %param.14) | copy-start | bytes 1540
  0.6 0.7 %copy-start.7 = (s32[128]{0:T(128)S(1)}, s32[128]{0:T(128)}, u32[]{:S(2)}) copy-start(s32[128]{0:T(128)} %param.15) | copy-start | bytes 1540
  1.3 0.9 %copy-start = (bf16[128,1024]{1,0:T(8,128)(2,1)S(1)}, bf16[128,1024]{1,0:T(8,128)(2,1)}, u32[]{:S(2)}) copy-start(bf16[128,1024]{1,0:T(8,128)(2,1)} %q_hbm.1) | copy-start | bytes 786436
  2.3 0.9 %copy-start.1 = (bf16[128,1024]{1,0:T(8,128)(2,1)S(1)}, bf16[128,1024]{1,0:T(8,128)(2,1)}, u32[]{:S(2)}) copy-start(bf16[128,1024]{1,0:T(8,128)(2,1)} %o_hbm.1) | copy-start | bytes 786436
  3.2 0.9 %copy-start.2 = (bf16[128,1024]{1,0:T(8,128)(2,1)S(1)}, bf16[128,1024]{1,0:T(8,128)(2,1)}, u32[]{:S(2)}) copy-start(bf16[128,1024]{1,0:T(8,128)(2,1)} %g_hbm.1) | copy-start | bytes 786436
  4.2 0.8 %copy-start.3 = (bf16[64,512]{1,0:T(8,128)(2,1)S(1)}, bf16[64,512]{1,0:T(8,128)(2,1)}, u32[]{:S(2)}) copy-start(bf16[64,512]{1,0:T(8,128)(2,1)} %k_hbm.1) | copy-start | bytes 196612
  5.0 0.8 %copy-start.4 = (bf16[64,512]{1,0:T(8,128)(2,1)S(1)}, bf16[64,512]{1,0:T(8,128)(2,1)}, u32[]{:S(2)}) copy-start(bf16[64,512]{1,0:T(8,128)(2,1)} %v_hbm.1) | copy-start | bytes 196612
  5.8 0.7 %copy-start.5 = (f32[8,128]{1,0:T(8,128)S(1)}, f32[8,128]{1,0:T(8,128)}, u32[]{:S(2)}) copy-start(f32[8,128]{1,0:T(8,128)} %lse_ref.1) | copy-start | bytes 12292

commit v2 on v1

--- a/solution.py
+++ b/solution.py
@@ -19,9 +19,9 @@
 def kernel(
     members, groups,
     q_hbm, k_hbm, v_hbm, o_hbm, g_hbm, lse_ref, order_ref, pos_ref,
-    dq_hbm, dk_hbm, dv_hbm,
+    dq_ref, dk_ref, dv_ref,
     q_buf, o_buf, g_buf, q_tall, g_tall, k_all, v_all, order_all,
-    lse_wide, dot_wide, ds_all, k_part, v_part, k_in, v_in, dq_buf, dk_buf, dv_buf,
+    lse_wide, dot_wide, ds_all, part, inbox,
     local_sem, send_kv, recv_kv, send_order, recv_order, send_grad, recv_grad,
 ):
     ctx, mine = lax.axis_index("ctx"), lax.axis_index("head")
@@ -81,14 +81,12 @@
             device_id_type=MESH,
         )
 
-    def grad_copy(which, member, head, sender, sender_head):
-        source = (k_part, v_part)[which]
-        target = (k_in, v_in)[which]
+    def grad_copy(member, head, sender, sender_head):
         return pltpu.make_async_remote_copy(
-            src_ref=source.at[member, half(head)],
-            dst_ref=target.at[sender, :, columns(sender_head)],
-            send_sem=send_grad.at[which, member, head],
-            recv_sem=recv_grad.at[which, sender, sender_head],
+            src_ref=part.at[member, head],
+            dst_ref=inbox.at[sender, sender_head],
+            send_sem=send_grad.at[member, head],
+            recv_sem=recv_grad.at[sender, sender_head],
             device_id=device(member, head),
             device_id_type=MESH,
         )
@@ -167,20 +165,20 @@
                 probs * (prob_grad - dot_wide[kv_head : kv_head + 1, :]) * scale
             ).astype(jnp.bfloat16)
             ds_all[kv_head, pl.ds(pl.multiple_of(member * rows, rows), rows), :] = score_grad
-            v_part[member, :, lanes] = dot(
-                probs.astype(jnp.bfloat16), grads, ((1,), (0,))
-            ).astype(jnp.bfloat16)
-            k_part[member, :, lanes] = dot(score_grad, queries, ((1,), (0,))).astype(jnp.bfloat16)
+            value_grad = dot(probs.astype(jnp.bfloat16), grads, ((1,), (0,)))
+            key_grad = dot(score_grad, queries, ((1,), (0,)))
+            for head in range(groups):
+                spot = slice(head * own, (head + 1) * own)
+                part[member, head, 0, :, lanes] = key_grad[spot].astype(jnp.bfloat16)
+                part[member, head, 1, :, lanes] = value_grad[spot].astype(jnp.bfloat16)
 
     for head_step in range(1, groups):
         for which in range(2):
             kv_copy(which, me, head_at(head_step), me, head_at(head_step)).wait_recv()
     block(me)
-    k_in[me, :, columns(mine)] = k_part[me, half(mine), :]
-    v_in[me, :, columns(mine)] = v_part[me, half(mine), :]
-    for head_step in range(1, groups):
-        for which in range(2):
-            grad_copy(which, me, head_at(head_step), me, mine).start()
+    inbox[me, mine] = part[me, mine]
+    for head_step in range(1, groups):
+        grad_copy(me, head_at(head_step), me, mine).start()
 
     def visit(step):
         member = member_at(step)
@@ -190,8 +188,7 @@
                 kv_copy(which, member, head_at(head_step), member, head_at(head_step)).wait_recv()
         block(member)
         for head_step in range(groups):
-            for which in range(2):
-                grad_copy(which, member, head_at(head_step), me, mine).start()
+            grad_copy(member, head_at(head_step), me, mine).start()
 
     loop(1, members, visit)
 
@@ -201,11 +198,9 @@
         update = dot(ds_all[kv_head], keys, ((0,), (0,))).astype(jnp.bfloat16)
         for place in range(group_size):
             head = kv_head * group_size + place
-            dq_buf[:, head * HEAD_DIM : (head + 1) * HEAD_DIM] = update[
+            dq_ref[:, head * HEAD_DIM : (head + 1) * HEAD_DIM] = update[
                 place * rows : (place + 1) * rows, :
             ]
-    dq_out = pltpu.make_async_copy(dq_buf, dq_hbm, local_sem.at[5])
-    dq_out.start()
 
     def sent(step):
         member = member_at(step)
@@ -213,25 +208,21 @@
         for head_step in range(groups):
             for which in range(2):
                 kv_copy(which, member, head_at(head_step), me, mine).wait_send()
-                grad_copy(which, member, head_at(head_step), me, mine).wait_send()
-                grad_copy(which, member, head_at(head_step), member, head_at(head_step)).wait_recv()
+            grad_copy(member, head_at(head_step), me, mine).wait_send()
+            grad_copy(member, head_at(head_step), member, head_at(head_step)).wait_recv()
 
     for head_step in range(1, groups):
         for which in range(2):
             kv_copy(which, me, head_at(head_step), me, mine).wait_send()
-            grad_copy(which, me, head_at(head_step), me, mine).wait_send()
-            grad_copy(which, me, head_at(head_step), me, head_at(head_step)).wait_recv()
+        grad_copy(me, head_at(head_step), me, mine).wait_send()
+        grad_copy(me, head_at(head_step), me, head_at(head_step)).wait_recv()
     loop(1, members, sent)
 
-    outs = []
-    for which, (inbox, buf, out) in enumerate(((k_in, dk_buf, dk_hbm), (v_in, dv_buf, dv_hbm))):
-        buf[...] = jnp.sum(inbox[...].astype(jnp.float32), axis=0).astype(jnp.bfloat16)
-        copy = pltpu.make_async_copy(buf, out, local_sem.at[6 + which])
-        copy.start()
-        outs.append(copy)
-    dq_out.wait()
-    for copy in outs:
-        copy.wait()
+    for head in range(groups):
+        lanes = slice(head * kv_columns, (head + 1) * kv_columns)
+        for which, out in enumerate((dk_ref, dv_ref)):
+            total = jnp.sum(inbox[:, head, which].astype(jnp.float32), axis=0)
+            out[:, lanes] = total.astype(jnp.bfloat16)
 
 
 def shards(
@@ -256,7 +247,7 @@
             jax.ShapeDtypeStruct(value_states.shape, bf16),
         ),
         in_specs=[anywhere] * 5 + [vmem] * 3,
-        out_specs=(anywhere,) * 3,
+        out_specs=(vmem,) * 3,
         scratch_shapes=[
             pltpu.VMEM((rows, head_columns), bf16),
             pltpu.VMEM((rows, head_columns), bf16),
@@ -269,23 +260,18 @@
             pltpu.VMEM((kv_local, wide), f32),
             pltpu.VMEM((kv_local, wide), f32),
             pltpu.VMEM((kv_local, members * rows, wide), bf16),
-            pltpu.VMEM((members, rows, kv_columns), bf16),
-            pltpu.VMEM((members, rows, kv_columns), bf16),
-            pltpu.VMEM((members, own, kv_total), bf16),
-            pltpu.VMEM((members, own, kv_total), bf16),
-            pltpu.VMEM((rows, head_columns), bf16),
-            pltpu.VMEM((own, kv_total), bf16),
-            pltpu.VMEM((own, kv_total), bf16),
-            dma((8,)),
+            pltpu.VMEM((members, groups, 2, own, kv_columns), bf16),
+            pltpu.VMEM((members, groups, 2, own, kv_columns), bf16),
+            dma((5,)),
             dma((2, members, groups)),
             dma((2, members, groups)),
             dma((members,)),
             dma((members,)),
-            dma((2, members, groups)),
-            dma((2, members, groups)),
+            dma((members, groups)),
+            dma((members, groups)),
         ],
         compiler_params=pltpu.CompilerParams(
-            collective_id=0, has_side_effects=True, vmem_limit_bytes=48 * 1024 * 1024
+            collective_id=0, has_side_effects=True, vmem_limit_bytes=67043328
         ),
     )(
         queries, key_states, value_states, attn_out, grad_out, log_sum_exp,

time: 39.3 us -> 35.7 us (0.908)
  local copies, waits for them, and re-layouts: 7.83 us -> 3.2 us
  Pallas kernels: 30.4 us -> 31.6 us
    unnamed x19 -> x7, local copies, waits for them, and re-layouts: 7.83 us -> 3.2 us
    pallas_call x1, Pallas kernels: 30.4 us -> 31.6 us  [shards(): pl.pallas_call(functools.partial(kernel, members, groups), out_shape=(jax...]
where the time goes in v2:
time: 35.7 us; the launch traced here: 35.4 us
  Pallas kernels  31.6 us (89%)
  local copies, waits for them, and re-layouts  3.2 us (9%)
  between operations  0.65 us (2%)
    pallas_call x1, Pallas kernels, shards(): pl.pallas_call(functools.partial(kernel, members, groups), out_shape=(jax...  31.6 us
    unnamed x7, local copies, waits for them, and re-layouts  3.2 us

profile of v2, /device:TPU:25, one launch (start us, length us, event | category | flops | bytes accessed | tf_op | source)
XLA Modules:
  0.0 35.4 jit_solution(6637632097045533987)
XLA Ops:
  0.6 31.6 %shard_map.103 = (bf16[128,1024]{1,0:T(8,128)(2,1)}, bf16[64,512]{1,0:T(8,128)(2,1)}, bf16[64,512]{1,0:T(8,128)(2,1)}) custom-call(bf16[128,1024]{1,0:T(8,128)(2,1)} %q_hbm.1, bf16[64,512]{1,0:T(8,128)(2,1)} %k_hbm.1, bf16[64,512]{1,0:T(8,128)(2,1)} %v_hbm.1, bf16[128,1024]{1,0:T(8,128)(2,1)} %o_hbm.1, bf16[128,1024]{1,0:T(8,128)(2,1)} %g_hbm.1, ...), custom_call_target="tpu_custom_call" | custom-call | tf_op jit(solution)/shard_map/pallas_call | solution.py:242
  32.2 0.0 copy-start.1
  32.2 1.7 %copy.14 = bf16[128,1024]{1,0:T(8,128)(2,1)} copy(bf16[128,1024]{1,0:T(8,128)(2,1)} %get-tuple-element.6) | data formatting | bytes 524288
  33.9 0.0 copy-done.1
  34.0 0.0 copy-start
  34.0 0.6 %copy.15 = bf16[64,512]{1,0:T(8,128)(2,1)} copy(bf16[64,512]{1,0:T(8,128)(2,1)S(1)} %copy-done.1) | data formatting | bytes 131072
  34.6 0.2 copy-done
  34.8 0.6 %copy.16 = bf16[64,512]{1,0:T(8,128)(2,1)} copy(bf16[64,512]{1,0:T(8,128)(2,1)S(1)} %copy-done) | data formatting | bytes 131072
Async XLA Ops:
  32.2 1.7 %copy-start.1 = (bf16[64,512]{1,0:T(8,128)(2,1)S(1)}, bf16[64,512]{1,0:T(8,128)(2,1)}, u32[]{:S(2)}) copy-start(bf16[64,512]{1,0:T(8,128)(2,1)} %get-tuple-element.7) | copy-start | bytes 196612
  34.0 0.9 %copy-start = (bf16[64,512]{1,0:T(8,128)(2,1)S(1)}, bf16[64,512]{1,0:T(8,128)(2,1)}, u32[]{:S(2)}) copy-start(bf16[64,512]{1,0:T(8,128)(2,1)} %get-tuple-element.8) | copy-start | bytes 196612
